TPU v7x, 256 devices: a whole 4x4x8 slice. The times are simulated.
256 devices in a mesh: section: 32 (over z_hi, y, core), dp: 8 (over z_lo, x).
Axes of the slice: x: 4, y: 4, z: 8 (z_hi: 4, z_lo: 2; z = z_hi * 2 + z_lo), core: 2. Of those that a mesh axis runs over, the one named last changes fastest.
Arguments:
- activations: bfloat16 [32, 64, 64, 4096], P('section', 'dp'), may hold values from -6 to 6
- out_grads: bfloat16 [32, 64, 64, 4096], P('section', 'dp'), may hold values from -6 to 6
- proj_in: bfloat16 [32, 2, 4096, 128], P('section'), may hold values from -0.09375 to 0.09375
- proj_out: bfloat16 [32, 2, 64, 4096], P('section'), may hold values from -0.09375 to 0.09375
- earlier_gram: float32 [8192, 8192], P('section', 'dp'), may hold values from -4 to 4, as said below
Outputs:
- gram: float32 [8192, 8192], P('section', 'dp')
Inputs may be any that keep to these rules, and one draw needn't show every extreme that they name: earlier_gram is symmetric.
All inputs are finite; a program needn't handle non-finite values.
Results may differ from a plain program's by a relative error of at most 0.0013.
Values sent between devices are 32-bit elements; how exact they have to be, the bound alone decides.
No kernel may reach another device: no remote copies, remote signals or barrier semaphores. Data moves between devices by JAX's collectives and lax.ppermute only.
A program may use at most 64 MiB of HBM per device.

v0:
```python
import math
import jax
import jax.numpy as jnp
from jax import lax
from jax.sharding import PartitionSpec as P

PROJ = 2
LEN = 64


def per_device(activations, out_grads, proj_in, proj_out, earlier_gram):
    layer_act = activations[0]
    layer_grad = out_grads[0]
    layer_in = proj_in[0]
    layer_out = proj_out[0]
    low_in = jnp.einsum(
        "etd,pdm->petm", layer_act, layer_in, preferred_element_type=jnp.float32
    ).astype(jnp.bfloat16)
    low_out = jnp.einsum(
        "pkd,etd->pekt", layer_out, layer_grad, preferred_element_type=jnp.float32
    ).astype(jnp.bfloat16)
    partial_terms = jnp.einsum(
        "pekt,petm->ekm", low_out, low_in, preferred_element_type=jnp.float32
    )
    local_count = partial_terms.shape[0]
    partial_terms = partial_terms.reshape(local_count, -1)
    n_layers = lax.axis_size("section")
    n_groups = lax.axis_size("dp")
    total_examples = local_count * n_groups
    scale = 1.0 / math.sqrt(LEN * n_layers * PROJ)
    row_width = earlier_gram.shape[0]
    col_width = earlier_gram.shape[1]
    row_start = lax.axis_index("section") * row_width
    col_start = lax.axis_index("dp") * col_width
    placed = jnp.zeros((total_examples, partial_terms.shape[1]), jnp.float32)
    placed = lax.dynamic_update_slice_in_dim(
        placed, partial_terms, lax.axis_index("dp") * local_count, 0
    )
    features = lax.psum(placed, ("section", "dp")) * scale
    row_block = lax.dynamic_slice_in_dim(features, row_start, row_width, 1)
    col_block = lax.dynamic_slice_in_dim(features, col_start, col_width, 1)
    outer = jnp.dot(row_block.T, col_block, precision=lax.Precision.HIGHEST)
    return earlier_gram + outer / total_examples


def solution(mesh):
    return jax.shard_map(
        per_device,
        mesh=mesh,
        in_specs=(
            P("section", "dp", None, None),
            P("section", "dp", None, None),
            P("section", None, None, None),
            P("section", None, None, None),
            P("section", "dp"),
        ),
        out_specs=P("section", "dp"),
        check_vma=False,
    )
```

profile of v0, /device:TPU:2, one launch (start us, length us, event | category | flops | bytes accessed | tf_op | source)
XLA Modules:
  0.0 292.4 jit_solution(597952820103288470)
XLA Ops:
  6.5 0.0 copy-start
  6.5 0.0 all-reduce.2.cloned.1.call-start
  6.5 4.8 %fusion.14 = bf16[2,8,64,64]{3,2,0,1:T(8,128)(2,1)S(1)} fusion(bf16[1,8,64,4096]{3,2,1,0:T(8,128)(2,1)} %param.6, bf16[1,2,64,4096]{3,2,1,0:T(8,128)(2,1)} %param.8), kind=kOutput, calls=%fused_computation.9 | convolution fusion | flops 536936448 | bytes 5373952 | tf_op jit(solution)/shard_map/pkd,etd->pekt/dot_general | solution.py:19
  11.3 0.0 copy-done
  11.3 3.6 %convolution_bitcast_fusion = f32[1,8,64,128]{3,2,1,0:T(8,128)S(1)} fusion(bf16[2,8,64,64]{3,2,0,1:T(8,128)(2,1)S(1)} %fusion.14, bf16[1,8,64,4096]{3,2,1,0:T(8,128)(2,1)} %param.5, bf16[1,2,4096,128]{3,2,1,0:T(8,128)(2,1)S(1)} %copy-done), kind=kOutput, calls=%fused_computation.10 | convolution fusion | flops 1090650112 | bytes 6684672 | tf_op jit(solution)/shard_map/pekt,petm->ekm/dot_general | solution.py:22
  15.0 1.5 broadcast_in_dim.3
  16.5 0.9 bitcast_dynamic-update-slice_fusion
  17.3 0.0 all-reduce.2.cloned.1.call-update
  17.4 0.0 copy-start.1
  17.4 264.4 %all-reduce.2.cloned.1.call-done = f32[64,8192]{1,0:T(8,128)} async-done(((f32[64,8192]{1,0:T(8,128)}), f32[64,8192]{1,0:T(8,128)}) %all-reduce.2.cloned.1.call-update) | async-done | bytes 2097168 | tf_op jit(solution)/shard_map/psum | solution.py:39
  281.8 1.8 broadcast_multiply_fusion
  283.5 0.0 copy-done.1
  283.5 2.0 fusion.5
Async XLA Ops:
  6.5 4.8 %copy-start = (bf16[1,2,4096,128]{3,2,1,0:T(8,128)(2,1)S(1)}, bf16[1,2,4096,128]{3,2,1,0:T(8,128)(2,1)}, u32[]{:S(2)}) copy-start(bf16[1,2,4096,128]{3,2,1,0:T(8,128)(2,1)} %param.7) | copy-start | bytes 6291460
  6.5 275.2 %all-reduce.2.cloned.1.call-start = ((), (), s32[]{:S(2)}) async-start(), calls=%async_computation | async-start | bytes 4194304 | tf_op jit(solution)/shard_map/psum | solution.py:39
  17.4 266.2 %copy-start.1 = (f32[256,1024]{1,0:T(8,128)S(1)}, f32[256,1024]{1,0:T(8,128)}, u32[]{:S(2)}) copy-start(f32[256,1024]{1,0:T(8,128)} %param.9) | copy-start | bytes 3145732
Sparse Core Ops, SparseCore 0:
  17.5 264.2 all-reduce.1
where the time goes:
time: 293 us; the launch traced here: 292 us
  waiting for transfers between devices  264 us (90%)
  between operations  13.4 us (5%)
  matrix products  10.4 us (4%)
    psum x1, waiting for transfers between devices, per_device(): features = lax.psum(placed, ('section', 'dp')) * scale  264 us
  transfers between devices with their start and end apart: 1, of which 1 were waited for; matrix products, arithmetic and copies ran while one was open for 0% of the time, Pallas kernels for 0%

commit v1 on v0

--- a/solution.py
+++ b/solution.py
@@ -36,7 +36,7 @@
     placed = lax.dynamic_update_slice_in_dim(
         placed, partial_terms, lax.axis_index("dp") * local_count, 0
     )
-    features = lax.psum(placed, ("section", "dp")) * scale
+    features = lax.psum(lax.psum(placed, "dp"), "section") * scale
     row_block = lax.dynamic_slice_in_dim(features, row_start, row_width, 1)
     col_block = lax.dynamic_slice_in_dim(features, col_start, col_width, 1)
     outer = jnp.dot(row_block.T, col_block, precision=lax.Precision.HIGHEST)

time: 293 us -> 414 us (1.41)
  waiting for transfers between devices: 264 us -> 385 us
    psum x1 -> x2, waiting for transfers between devices: 264 us -> 385 us  [per_device(): features = lax.psum(lax.psum(placed, 'dp'), 'section') * scale]
  transfers between devices with their start and end apart: 1 -> 2, of which waited for: 1 -> 2; matrix products, arithmetic and copies ran while one was open for 0% -> 0% of each run, Pallas kernels for 0% -> 0%
where the time goes in v1:
time: 414 us; the launch traced here: 413 us
  waiting for transfers between devices  385 us (93%)
  between operations  13.4 us (3%)
  matrix products  10.4 us (3%)
    psum x2, waiting for transfers between devices, per_device(): features = lax.psum(lax.psum(placed, 'dp'), 'section') * scale  385 us
  transfers between devices with their start and end apart: 2, of which 2 were waited for; matrix products, arithmetic and copies ran while one was open for 0% of the time, Pallas kernels for 0%

profile of v1, /device:TPU:2, one launch (start us, length us, event | category | flops | bytes accessed | tf_op | source)
XLA Modules:
  0.0 413.2 jit_solution(18237705975545066314)
XLA Ops:
  6.5 0.0 copy-start
  6.5 0.0 all-reduce.3.cloned.1.call-start
  6.5 4.8 %fusion.14 = bf16[2,8,64,64]{3,2,0,1:T(8,128)(2,1)S(1)} fusion(bf16[1,8,64,4096]{3,2,1,0:T(8,128)(2,1)} %param.6, bf16[1,2,64,4096]{3,2,1,0:T(8,128)(2,1)} %param.8), kind=kOutput, calls=%fused_computation.9 | convolution fusion | flops 536936448 | bytes 5373952 | tf_op jit(solution)/shard_map/pkd,etd->pekt/dot_general | solution.py:19
  11.3 0.0 copy-done
  11.3 3.6 convolution_bitcast_fusion
  15.0 1.5 broadcast_in_dim.3
  16.5 0.9 bitcast_dynamic-update-slice_fusion
  17.3 0.0 all-reduce.3.cloned.1.call-update
  17.3 0.0 all-reduce.5.cloned.1.call-start
  17.4 89.8 %all-reduce.3.cloned.1.call-done = f32[64,8192]{1,0:T(8,128)} async-done(((f32[64,8192]{1,0:T(8,128)}), f32[64,8192]{1,0:T(8,128)}) %all-reduce.3.cloned.1.call-update) | async-done | bytes 2097168 | tf_op jit(solution)/shard_map/psum | solution.py:39
  107.2 0.0 all-reduce.5.cloned.1.call-update
  107.2 0.0 copy-start.1
  107.3 295.3 %all-reduce.5.cloned.1.call-done = f32[64,8192]{1,0:T(8,128)} async-done(((f32[64,8192]{1,0:T(8,128)}), f32[64,8192]{1,0:T(8,128)}) %all-reduce.5.cloned.1.call-update) | async-done | bytes 2097168 | tf_op jit(solution)/shard_map/psum | solution.py:39
  402.6 1.8 broadcast_multiply_fusion
  404.4 0.0 copy-done.1
  404.4 2.0 fusion.5
Async XLA Ops:
  6.5 4.8 %copy-start = (bf16[1,2,4096,128]{3,2,1,0:T(8,128)(2,1)S(1)}, bf16[1,2,4096,128]{3,2,1,0:T(8,128)(2,1)}, u32[]{:S(2)}) copy-start(bf16[1,2,4096,128]{3,2,1,0:T(8,128)(2,1)} %param.7) | copy-start | bytes 6291460
  6.5 100.7 %all-reduce.3.cloned.1.call-start = ((), (), s32[]{:S(2)}) async-start(), calls=%async_computation | async-start | bytes 4194304 | tf_op jit(solution)/shard_map/psum | solution.py:39
  17.3 385.3 %all-reduce.5.cloned.1.call-start = ((), (), s32[]{:S(2)}) async-start(), calls=%async_computation.1 | async-start | bytes 4194304 | tf_op jit(solution)/shard_map/psum | solution.py:39
  107.2 297.1 %copy-start.1 = (f32[256,1024]{1,0:T(8,128)S(1)}, f32[256,1024]{1,0:T(8,128)}, u32[]{:S(2)}) copy-start(f32[256,1024]{1,0:T(8,128)} %param.9) | copy-start | bytes 3145732
Sparse Core Ops, SparseCore 0:
  17.5 89.7 all-reduce.2
  109.8 292.7 all-reduce.4
